TPU v7x, 512 devices: a whole 4x8x8 slice. The times are simulated.
512 devices in a mesh: row: 128 (over z_hi, y, x, core), col: 4 (over z_lo).
Axes of the slice: x: 4, y: 8, z: 8 (z_hi: 2, z_lo: 4; z = z_hi * 4 + z_lo), core: 2. Of those that a mesh axis runs over, the one named last changes fastest.
Arguments:
- coeffs: float32 [32, 512, 512], P('col', 'row'), may hold values from -0.01171875 to 0.01171875
- constraint_coeffs: float32 [2, 32], replicated, may hold values from 0.3 to 1
- alpha: float32 [1], replicated, may hold values from 0.95 to 1.05
- coset_shift: float32 [1], replicated, may hold values from 0.2 to 0.8
Outputs:
- evaluations: float32 [2, 32, 2048, 512], P(None, 'col', 'row')
- quotient: float32 [2, 2048, 512], P(None, 'row', 'col')
All inputs are finite; a program needn't handle non-finite values.
Results may differ from a plain program's by a relative error of at most 0.000082.
Values sent between devices are 32-bit elements; how exact they have to be, the bound alone decides.
A program may use at most 64 MiB of HBM per device.

v0:
```python
import math

import jax
import jax.numpy as jnp
import ml_dtypes
import numpy as np
from jax import lax
from jax.experimental import pallas as pl
from jax.experimental.pallas import tpu as pltpu
from jax.sharding import PartitionSpec as P

MESH = pl.DeviceIdType.MESH
TAU = 2.0 * math.pi

COLS = 8
GROUPS = 4
ROWS = 128
HALF = 64
TILES = 8
K2 = 512
POINTS = 512
BLOCK = 16
STEP = 4
PEERS = HALF - 1
BARRIER = PEERS + 1 + (GROUPS - 1) + GROUPS


def split_table(table):
    high = table.astype(np.float32).astype(ml_dtypes.bfloat16)
    low = (table - high.astype(np.float64)).astype(np.float32).astype(ml_dtypes.bfloat16)
    return high, low


def inner_table():
    k2 = np.arange(K2)[:, None]
    point = np.arange(1024)[None, :]
    angle = (k2 * point % 2048) * (TAU / 2048)
    cosine = np.cos(angle).reshape(K2, TILES, 128)
    sine = np.sin(angle).reshape(K2, TILES, 128)
    return split_table(np.concatenate((cosine, sine), axis=2).transpose(1, 0, 2))


def outer_table():
    device = np.arange(HALF)[:, None, None]
    half = np.arange(2)[None, :, None]
    low = np.arange(4)[None, None, :]
    k1 = (256 * half + 4 * device + low).reshape(POINTS, 1)
    angle = (k1 * np.arange(POINTS)[None, :] % POINTS) * (TAU / POINTS)
    return split_table(np.concatenate((np.cos(angle), np.sin(angle)), axis=1))


def split(values):
    high = values.astype(jnp.bfloat16)
    return high, (values - high.astype(jnp.float32)).astype(jnp.bfloat16)


def dot(left, right):
    return jnp.dot(left, right, preferred_element_type=jnp.float32)


def swap_groups(pieces):
    lane = lax.broadcasted_iota(jnp.int32, pieces[0].shape, pieces[0].ndim - 1)
    axis = pieces[0].ndim - 1
    pieces = list(pieces)
    for bit in (4, 2, 1):
        keep = (lane // (16 * bit)) % 2 == 0
        for first in range(8):
            if first & bit:
                continue
            a, b = pieces[first], pieces[first + bit]
            pieces[first] = jnp.where(keep, a, pltpu.roll(b, 16 * bit, axis))
            pieces[first + bit] = jnp.where(keep, pltpu.roll(a, 128 - 16 * bit, axis), b)
    return pieces


def kernel(
    coeffs,
    constraint,
    alpha,
    coset,
    in_high,
    in_low,
    out_high,
    out_low,
    evaluations,
    quotient,
    both,
    ih,
    il,
    oh,
    ol,
    x_high,
    x_low,
    twist,
    outgoing,
    incoming,
    values,
    part_out,
    part_in,
    edge_out,
    edge_in,
    table_sem,
    pair_sem,
    all_sem,
    part_sem,
    edge_sem,
    store_sem,
):
    row = lax.axis_index("row")
    col = lax.axis_index("col")
    half = row // HALF
    place = row % HALF
    tile = place // 8
    core = place % 2
    base = half * HALF
    previous = (row + ROWS - 1) % ROWS
    following = (row + 1) % ROWS
    partner = (row + HALF) % ROWS

    barrier = pltpu.get_barrier_semaphore()

    def greet(device):
        pl.semaphore_signal(barrier, inc=1, device_id=device, device_id_type=MESH)

    greet((partner, col))

    @pl.loop(1, HALF)
    def _(i):
        greet((base + (place + i) % HALF, col))

    for i in range(1, GROUPS):
        greet((row, (col + i) % GROUPS))
    for i in range(GROUPS):
        greet((following, i))

    loads = [
        pltpu.make_async_copy(source, target, table_sem.at[i])
        for i, (source, target) in enumerate(
            ((in_high, ih), (in_low, il), (out_high, oh), (out_low, ol))
        )
    ]
    for load in loads:
        load.start()

    shift = coset[0]
    both[half] = coeffs[...]
    k2 = lax.broadcasted_iota(jnp.int32, (1, K2), 1)
    phase = k2.astype(jnp.float32) * (shift * (TAU / 2048))
    sign = (1 - 2 * ((k2 % 2) * half)).astype(jnp.float32)
    phase_cos = jnp.cos(phase) * sign
    phase_sin = jnp.sin(phase) * sign

    sub = lax.broadcasted_iota(jnp.int32, (8, 1024), 0)
    k1 = 256 * (sub // 4) + 4 * place + sub % 4
    point = 1024 * half + lax.broadcasted_iota(jnp.int32, (8, 1024), 1)
    k1_f = k1.astype(jnp.float32)
    angle = ((k1 * point).astype(jnp.float32) + k1_f * shift) * (TAU / 1048576)
    twist_cos = jnp.cos(angle)
    twist_sin = jnp.sin(angle)
    for t in range(TILES):
        twist[t, 0] = twist_cos[:, 128 * t : 128 * t + 128]
        twist[t, 1] = twist_sin[:, 128 * t : 128 * t + 128]

    pl.semaphore_wait(barrier, BARRIER)

    pair = pltpu.make_async_remote_copy(
        src_ref=coeffs,
        dst_ref=both.at[half],
        send_sem=pair_sem.at[0],
        recv_sem=pair_sem.at[1],
        device_id=(partner, col),
        device_id_type=MESH,
    )
    pair.start()
    pair.wait()

    x = jnp.concatenate((both[0], both[1]), axis=1).reshape(64, K2)
    x = jnp.concatenate((x * phase_cos, x * phase_sin), axis=0)
    high, low = split(x)
    x_high[...] = high
    x_low[...] = low
    loads[0].wait()
    loads[1].wait()

    def send(device):
        return pltpu.make_async_remote_copy(
            src_ref=outgoing.at[device],
            dst_ref=incoming.at[place],
            send_sem=all_sem.at[0],
            recv_sem=all_sem.at[1],
            device_id=(base + device, col),
            device_id_type=MESH,
        )

    @pl.loop(0, TILES)
    def _(i):
        offset = (i + 1) // 2 * (2 * ((i + 1) % 2) - 1)
        t = (tile + 4 + offset * (1 - 2 * core) + 8) % TILES
        ah, al = x_high[...], x_low[...]
        bh, bl = ih[t], il[t]
        y = dot(ah, bh) + (dot(al, bh) + dot(ah, bl))
        real = (y[:64, :128] - y[64:, 128:]).reshape(COLS, 8, 128)
        imag = (y[:64, 128:] + y[64:, :128]).reshape(COLS, 8, 128)
        cosine, sine = twist[t, 0][None], twist[t, 1][None]
        turned_real = real * cosine - imag * sine
        turned_imag = real * sine + imag * cosine
        swapped_real = swap_groups([turned_real[c] for c in range(COLS)])
        swapped_imag = swap_groups([turned_imag[c] for c in range(COLS)])
        for d in range(8):
            outgoing[8 * t + d, :, :128] = swapped_real[d]
            outgoing[8 * t + d, :, 128:] = swapped_imag[d]

        @pl.loop(0, 8)
        def _(j):
            device = 8 * t + (place + j) % 8

            @pl.when(device != place)
            def _():
                send(device).start()

    incoming[place] = outgoing[place]
    everything = pltpu.make_async_remote_copy(
        src_ref=outgoing.at[pl.ds(0, PEERS)],
        dst_ref=incoming.at[pl.ds(0, PEERS)],
        send_sem=all_sem.at[0],
        recv_sem=all_sem.at[1],
        device_id=(partner, col),
        device_id_type=MESH,
    )
    loads[2].wait()
    loads[3].wait()
    everything.wait_recv()

    held = incoming[...].reshape(POINTS, 256).T
    rh, rl = split(held)
    th, tl = oh[...], ol[...]
    v = dot(rh, th) + (dot(rl, th) + dot(rh, tl))
    real = (v[:128, :POINTS] - v[128:, POINTS:]).reshape(COLS, BLOCK, POINTS)
    imag = (v[:128, POINTS:] + v[128:, :POINTS]).reshape(COLS, BLOCK, POINTS)
    values[0] = real
    values[1] = imag
    store = pltpu.make_async_copy(values, evaluations, store_sem)
    store.start()

    a1 = alpha[0]
    a2 = a1 * a1
    a4 = a2 * a2
    a8 = a4 * a4
    weight = jnp.where(col % 2 == 1, a8, 1.0) * jnp.where(col // 2 == 1, a8 * a8, 1.0)
    ahead_real = ahead_imag = sum_real = sum_imag = 0.0
    for c in range(COLS):
        quad = constraint[0, COLS * col + c]
        linear = constraint[1, COLS * col + c]
        vr, vi = real[c], imag[c]
        ahead_real += weight * vr
        ahead_imag += weight * vi
        sum_real += weight * (quad * (vr * vr - vi * vi) + linear * vr)
        sum_imag += weight * (quad * (2.0 * vr * vi) + linear * vi)
        weight = weight * a1

    none = jnp.zeros((STEP, POINTS), jnp.float32)
    sum_real = jnp.concatenate((ahead_real[STEP:], none), axis=0) - sum_real
    sum_imag = jnp.concatenate((ahead_imag[STEP:], none), axis=0) - sum_imag
    edge = jnp.concatenate((ahead_real[:STEP], ahead_imag[:STEP]), axis=0)
    edge = jnp.where(row == 0, pltpu.roll(edge, POINTS - 1, 1), edge)
    for q in range(GROUPS):
        edge_out[q] = edge[:, 128 * q : 128 * q + 128]
        part_out[q, 0] = sum_real[:, 128 * q : 128 * q + 128]
        part_out[q, 1] = sum_imag[:, 128 * q : 128 * q + 128]

    def send_part(target):
        return pltpu.make_async_remote_copy(
            src_ref=part_out.at[target],
            dst_ref=part_in.at[col],
            send_sem=part_sem.at[0],
            recv_sem=part_sem.at[1],
            device_id=(row, target),
            device_id_type=MESH,
        )

    for i in range(1, GROUPS):
        send_part((col + i) % GROUPS).start()
    for q in range(GROUPS):
        pltpu.make_async_remote_copy(
            src_ref=edge_out.at[q],
            dst_ref=edge_in.at[col],
            send_sem=edge_sem.at[0],
            recv_sem=edge_sem.at[1],
            device_id=(previous, q),
            device_id_type=MESH,
        ).start()
    part_in[col] = part_out[col]

    point = lax.broadcasted_iota(jnp.int32, (BLOCK, 128), 0) % STEP
    theta = (shift + point.astype(jnp.float32)) * (TAU / STEP)
    van_real = jnp.cos(theta) - 1.0
    van_imag = jnp.sin(theta)
    denominator = van_real * van_real + van_imag * van_imag

    parts = pltpu.make_async_remote_copy(
        src_ref=part_out.at[pl.ds(0, GROUPS - 1)],
        dst_ref=part_in.at[pl.ds(0, GROUPS - 1)],
        send_sem=part_sem.at[0],
        recv_sem=part_sem.at[1],
        device_id=(partner, col),
        device_id_type=MESH,
    )
    edges = pltpu.make_async_remote_copy(
        src_ref=edge_out,
        dst_ref=edge_in,
        send_sem=edge_sem.at[0],
        recv_sem=edge_sem.at[1],
        device_id=(partner, col),
        device_id_type=MESH,
    )
    parts.wait_recv()
    edges.wait_recv()
    part = (part_in[0] + part_in[1]) + (part_in[2] + part_in[3])
    edge = (edge_in[0] + edge_in[1]) + (edge_in[2] + edge_in[3])
    none = jnp.zeros((BLOCK - STEP, 128), jnp.float32)
    num_real = part[0] + jnp.concatenate((none, edge[:STEP]), axis=0)
    num_imag = part[1] + jnp.concatenate((none, edge[STEP:]), axis=0)
    quotient[0] = (num_real * van_real + num_imag * van_imag) / denominator
    quotient[1] = (num_imag * van_real - num_real * van_imag) / denominator

    everything.wait_send()
    parts.wait_send()
    edges.wait_send()
    store.wait()


def per_device(coeffs, constraint_coeffs, alpha, coset_shift):
    tables = inner_table() + outer_table()
    any_space = pl.BlockSpec(memory_space=pl.ANY)
    vmem = pl.BlockSpec(memory_space=pltpu.VMEM)
    smem = pl.BlockSpec(memory_space=pltpu.SMEM)
    f32 = jnp.float32
    bf16 = jnp.bfloat16
    return pl.pallas_call(
        kernel,
        out_shape=(
            jax.ShapeDtypeStruct((2, COLS, BLOCK, POINTS), f32),
            jax.ShapeDtypeStruct((2, BLOCK, 128), f32),
        ),
        in_specs=[vmem, smem, smem, smem] + [any_space] * 4,
        out_specs=(any_space, vmem),
        scratch_shapes=[
            pltpu.VMEM((2, COLS, 4, K2), f32),
            pltpu.VMEM((TILES, K2, 256), bf16),
            pltpu.VMEM((TILES, K2, 256), bf16),
            pltpu.VMEM((POINTS, 2 * POINTS), bf16),
            pltpu.VMEM((POINTS, 2 * POINTS), bf16),
            pltpu.VMEM((128, K2), bf16),
            pltpu.VMEM((128, K2), bf16),
            pltpu.VMEM((TILES, 2, 8, 128), f32),
            pltpu.VMEM((HALF, 8, 256), f32),
            pltpu.VMEM((HALF, 8, 256), f32),
            pltpu.VMEM((2, COLS, BLOCK, POINTS), f32),
            pltpu.VMEM((GROUPS, 2, BLOCK, 128), f32),
            pltpu.VMEM((GROUPS, 2, BLOCK, 128), f32),
            pltpu.VMEM((GROUPS, 8, 128), f32),
            pltpu.VMEM((GROUPS, 8, 128), f32),
            pltpu.SemaphoreType.DMA((4,)),
            pltpu.SemaphoreType.DMA((2,)),
            pltpu.SemaphoreType.DMA((2,)),
            pltpu.SemaphoreType.DMA((2,)),
            pltpu.SemaphoreType.DMA((2,)),
            pltpu.SemaphoreType.DMA,
        ],
        compiler_params=pltpu.CompilerParams(
            collective_id=0, has_side_effects=True, vmem_limit_bytes=48 * 1024 * 1024
        ),
    )(coeffs, constraint_coeffs, alpha, coset_shift, *tables)


def solution(mesh):
    in_specs = (P("col", "row", None), P(), P(), P())
    out_specs = (P(None, "col", "row", None), P(None, "row", "col"))
    return jax.shard_map(
        per_device, mesh=mesh, in_specs=in_specs, out_specs=out_specs, check_vma=False
    )
```

profile of v0, /device:TPU:1, one launch (start us, length us, event | category | flops | bytes accessed | tf_op | source)
XLA Modules:
  0.0 52.9 jit_solution(3743720364937430660)
XLA Ops:
  1.9 0.0 copy-start
  1.9 1.6 %copy-done = bf16[8,512,256]{2,1,0:T(8,128)(2,1)S(1)} copy-done((bf16[8,512,256]{2,1,0:T(8,128)(2,1)S(1)}, bf16[8,512,256]{2,1,0:T(8,128)(2,1)}, u32[]{:S(2)}) %copy-start) | copy-done | bytes 2097176
  3.5 0.0 copy-start.1
  3.5 1.2 %copy-done.1 = bf16[512,1024]{1,0:T(8,128)(2,1)S(1)} copy-done((bf16[512,1024]{1,0:T(8,128)(2,1)S(1)}, bf16[512,1024]{1,0:T(8,128)(2,1)}, u32[]{:S(2)}) %copy-start.1) | copy-done | bytes 1048600
  4.7 0.0 copy-start.2
  4.7 1.2 %copy-done.2 = bf16[512,1024]{1,0:T(8,128)(2,1)S(1)} copy-done((bf16[512,1024]{1,0:T(8,128)(2,1)S(1)}, bf16[512,1024]{1,0:T(8,128)(2,1)}, u32[]{:S(2)}) %copy-start.2) | copy-done | bytes 1048600
  6.0 0.0 copy-start.3
  6.0 0.8 %copy-done.3 = f32[8,4,512]{2,1,0:T(4,128)S(1)} copy-done((f32[8,4,512]{2,1,0:T(4,128)S(1)}, f32[8,4,512]{2,1,0:T(4,128)}, u32[]{:S(2)}) %copy-start.3) | copy-done | bytes 65560
  6.8 0.0 copy-start.4
  6.8 0.7 %copy-done.4 = f32[2,32]{1,0:T(2,128)S(1)} copy-done((f32[2,32]{1,0:T(2,128)S(1)}, f32[2,32]{1,0:T(2,128)}, u32[]{:S(2)}) %copy-start.4) | copy-done | bytes 280
  7.5 44.0 %shard_map.95 = (f32[2,8,16,512]{3,2,1,0:T(8,128)S(1)}, f32[2,16,128]{2,1,0:T(8,128)S(1)}) custom-call(f32[8,4,512]{2,1,0:T(4,128)S(1)} %copy-done.3, f32[2,32]{1,0:T(2,128)S(1)} %copy-done.4, f32[1]{0:T(128)S(6)} %copy.12.alpha, f32[1]{0:T(128)S(6)} %copy.13.coset, bf16[8,512,256]{2,1,0:T(8,128)(2,1)S(1)} %copy-done, ...), custom_call_target="tpu_custom_call" | custom-call | tf_op jit(solution)/shard_map/pallas_call | solution.py:339
  51.5 0.8 %copy.14 = f32[2,8,16,512]{3,2,1,0:T(8,128)} copy(f32[2,8,16,512]{3,2,1,0:T(8,128)S(1)} %get-tuple-element.4) | data formatting | bytes 1048576
  52.3 0.6 %copy.15 = f32[2,16,128]{2,1,0:T(8,128)} copy(f32[2,16,128]{2,1,0:T(8,128)S(1)} %get-tuple-element.5) | data formatting | bytes 32768
Async XLA Ops:
  1.9 1.6 %copy-start = (bf16[8,512,256]{2,1,0:T(8,128)(2,1)S(1)}, bf16[8,512,256]{2,1,0:T(8,128)(2,1)}, u32[]{:S(2)}) copy-start(bf16[8,512,256]{2,1,0:T(8,128)(2,1)} %constant.8.clone.in_high) | copy-start | bytes 6291460
  3.5 1.2 %copy-start.1 = (bf16[512,1024]{1,0:T(8,128)(2,1)S(1)}, bf16[512,1024]{1,0:T(8,128)(2,1)}, u32[]{:S(2)}) copy-start(bf16[512,1024]{1,0:T(8,128)(2,1)} %constant.11.clone.out_low) | copy-start | bytes 3145732
  4.7 1.2 %copy-start.2 = (bf16[512,1024]{1,0:T(8,128)(2,1)S(1)}, bf16[512,1024]{1,0:T(8,128)(2,1)}, u32[]{:S(2)}) copy-start(bf16[512,1024]{1,0:T(8,128)(2,1)} %constant.10.clone.out_high) | copy-start | bytes 3145732
  6.0 0.8 %copy-start.3 = (f32[8,4,512]{2,1,0:T(4,128)S(1)}, f32[8,4,512]{2,1,0:T(4,128)}, u32[]{:S(2)}) copy-start(f32[8,4,512]{2,1,0:T(4,128)} %coeffs.1) | copy-start | bytes 196612
  6.8 0.7 %copy-start.4 = (f32[2,32]{1,0:T(2,128)S(1)}, f32[2,32]{1,0:T(2,128)}, u32[]{:S(2)}) copy-start(f32[2,32]{1,0:T(2,128)} %constraint.1) | copy-start | bytes 772
where the time goes:
time: 53.2 us; the launch traced here: 52.9 us
  Pallas kernels  44 us (83%)
  local copies, waits for them, and re-layouts  6.95 us (13%)
  between operations  1.94 us (4%)
    pallas_call x1, Pallas kernels, per_device(): pl.pallas_call(kernel, out_shape=(jax.ShapeDtypeStruct((2, COLS, BLOCK, P...  44 us
    unnamed x12, local copies, waits for them, and re-layouts  6.95 us

commit v1 on v0

--- a/solution.py
+++ b/solution.py
@@ -37,16 +37,20 @@
     angle = (k2 * point % 2048) * (TAU / 2048)
     cosine = np.cos(angle).reshape(K2, TILES, 128)
     sine = np.sin(angle).reshape(K2, TILES, 128)
-    return split_table(np.concatenate((cosine, sine), axis=2).transpose(1, 0, 2))
+    table = np.concatenate((cosine, sine), axis=2).transpose(1, 0, 2)
+    return np.stack(split_table(table), axis=1)
 
 
 def outer_table():
-    device = np.arange(HALF)[:, None, None]
-    half = np.arange(2)[None, :, None]
-    low = np.arange(4)[None, None, :]
-    k1 = (256 * half + 4 * device + low).reshape(POINTS, 1)
-    angle = (k1 * np.arange(POINTS)[None, :] % POINTS) * (TAU / POINTS)
-    return split_table(np.concatenate((np.cos(angle), np.sin(angle)), axis=1))
+    place = np.arange(HALF)[:, None]
+    low = np.arange(4)[None, :]
+    k1 = np.stack([256 * part + 4 * place + low for part in range(2)])
+    angle = (k1[..., None] * np.arange(POINTS) % POINTS) * (TAU / POINTS)
+    cosine, sine = np.cos(angle), np.sin(angle)
+    from_real = np.concatenate((cosine, sine), axis=3)
+    from_imag = np.concatenate((-sine, cosine), axis=3)
+    table = np.stack((from_real, from_imag), axis=2).reshape(2, 2 * 256, 2 * POINTS)
+    return np.stack(split_table(table), axis=1)
 
 
 def split(values):
@@ -78,33 +82,29 @@
     constraint,
     alpha,
     coset,
-    in_high,
-    in_low,
-    out_high,
-    out_low,
+    inner_hbm,
+    outer_hbm,
     evaluations,
     quotient,
-    both,
-    ih,
-    il,
-    oh,
-    ol,
-    x_high,
-    x_low,
+    own,
+    other,
+    inner,
+    outer,
+    x_split,
     twist,
     outgoing,
     incoming,
-    values,
     part_out,
     part_in,
     edge_out,
     edge_in,
     table_sem,
+    own_sem,
     pair_sem,
-    all_sem,
+    send_sem,
+    recv_sem,
     part_sem,
     edge_sem,
-    store_sem,
 ):
     row = lax.axis_index("row")
     col = lax.axis_index("col")
@@ -133,17 +133,24 @@
     for i in range(GROUPS):
         greet((following, i))
 
-    loads = [
-        pltpu.make_async_copy(source, target, table_sem.at[i])
-        for i, (source, target) in enumerate(
-            ((in_high, ih), (in_low, il), (out_high, oh), (out_low, ol))
-        )
-    ]
-    for load in loads:
-        load.start()
+    def tile_of(i):
+        offset = (i + 1) // 2 * (2 * ((i + 1) % 2) - 1)
+        return (tile + 4 + offset * (1 - 2 * core) + 8) % TILES
+
+    def load_tile(t):
+        return pltpu.make_async_copy(inner_hbm.at[t], inner.at[t], table_sem.at[t])
+
+    load_own = pltpu.make_async_copy(coeffs, own, own_sem)
+    load_own.start()
+
+    @pl.loop(0, TILES)
+    def _(i):
+        load_tile(tile_of(i)).start()
+
+    load_outer = pltpu.make_async_copy(outer_hbm, outer, table_sem.at[TILES])
+    load_outer.start()
 
     shift = coset[0]
-    both[half] = coeffs[...]
     k2 = lax.broadcasted_iota(jnp.int32, (1, K2), 1)
     phase = k2.astype(jnp.float32) * (shift * (TAU / 2048))
     sign = (1 - 2 * ((k2 % 2) * half)).astype(jnp.float32)
@@ -151,96 +158,119 @@
     phase_sin = jnp.sin(phase) * sign
 
     sub = lax.broadcasted_iota(jnp.int32, (8, 1024), 0)
-    k1 = 256 * (sub // 4) + 4 * place + sub % 4
+    k1 = 256 * ((half + sub // 4) % 2) + 4 * place + sub % 4
     point = 1024 * half + lax.broadcasted_iota(jnp.int32, (8, 1024), 1)
     k1_f = k1.astype(jnp.float32)
     angle = ((k1 * point).astype(jnp.float32) + k1_f * shift) * (TAU / 1048576)
-    twist_cos = jnp.cos(angle)
-    twist_sin = jnp.sin(angle)
-    for t in range(TILES):
-        twist[t, 0] = twist_cos[:, 128 * t : 128 * t + 128]
-        twist[t, 1] = twist_sin[:, 128 * t : 128 * t + 128]
-
+    cosine, sine = jnp.cos(angle), jnp.sin(angle)
+    cosine_turned, sine_turned = pltpu.roll(cosine, 4, 0), pltpu.roll(sine, 4, 0)
+    upper = sub < 4
+    pairs = (
+        (jnp.where(upper, cosine, cosine_turned), jnp.where(upper, -sine, sine_turned)),
+        (jnp.where(upper, cosine_turned, cosine), jnp.where(upper, -sine_turned, sine)),
+    )
+    for p in range(2):
+        for t in range(TILES):
+            twist[p, t, 0] = pairs[p][0][:, 128 * t : 128 * t + 128]
+            twist[p, t, 1] = pairs[p][1][:, 128 * t : 128 * t + 128]
+
+    def prepare(p, source):
+        x = source[...]
+        x = jnp.concatenate((x * phase_cos, x * phase_sin), axis=1).reshape(64, K2)
+        high, low = split(x)
+        x_split[p, 0] = high
+        x_split[p, 1] = low
+
+    load_own.wait()
+    prepare(0, own)
     pl.semaphore_wait(barrier, BARRIER)
 
     pair = pltpu.make_async_remote_copy(
         src_ref=coeffs,
-        dst_ref=both.at[half],
+        dst_ref=other,
         send_sem=pair_sem.at[0],
         recv_sem=pair_sem.at[1],
         device_id=(partner, col),
         device_id_type=MESH,
     )
     pair.start()
-    pair.wait()
-
-    x = jnp.concatenate((both[0], both[1]), axis=1).reshape(64, K2)
-    x = jnp.concatenate((x * phase_cos, x * phase_sin), axis=0)
-    high, low = split(x)
-    x_high[...] = high
-    x_low[...] = low
-    loads[0].wait()
-    loads[1].wait()
-
-    def send(device):
+
+    def send(p, device):
         return pltpu.make_async_remote_copy(
-            src_ref=outgoing.at[device],
-            dst_ref=incoming.at[place],
-            send_sem=all_sem.at[0],
-            recv_sem=all_sem.at[1],
+            src_ref=outgoing.at[p, device],
+            dst_ref=incoming.at[(half + p) % 2, place],
+            send_sem=send_sem.at[p],
+            recv_sem=recv_sem.at[p],
             device_id=(base + device, col),
             device_id_type=MESH,
         )
 
-    @pl.loop(0, TILES)
-    def _(i):
-        offset = (i + 1) // 2 * (2 * ((i + 1) % 2) - 1)
-        t = (tile + 4 + offset * (1 - 2 * core) + 8) % TILES
-        ah, al = x_high[...], x_low[...]
-        bh, bl = ih[t], il[t]
+    def whole(p):
+        return pltpu.make_async_remote_copy(
+            src_ref=outgoing.at[p, pl.ds(0, PEERS)],
+            dst_ref=incoming.at[(half + p) % 2, pl.ds(0, PEERS)],
+            send_sem=send_sem.at[p],
+            recv_sem=recv_sem.at[p],
+            device_id=(partner, col),
+            device_id_type=MESH,
+        )
+
+    minus = jnp.where(lax.broadcasted_iota(jnp.int32, (1, 8, 128), 1) < 4, -1.0, 1.0)
+
+    def run_tile(p, t):
+        ah, al = x_split[p, 0], x_split[p, 1]
+        bh, bl = inner[t, 0], inner[t, 1]
         y = dot(ah, bh) + (dot(al, bh) + dot(ah, bl))
-        real = (y[:64, :128] - y[64:, 128:]).reshape(COLS, 8, 128)
-        imag = (y[:64, 128:] + y[64:, :128]).reshape(COLS, 8, 128)
-        cosine, sine = twist[t, 0][None], twist[t, 1][None]
-        turned_real = real * cosine - imag * sine
-        turned_imag = real * sine + imag * cosine
-        swapped_real = swap_groups([turned_real[c] for c in range(COLS)])
-        swapped_imag = swap_groups([turned_imag[c] for c in range(COLS)])
+        z = y[:, :128].reshape(COLS, 8, 128)
+        z = z + minus * pltpu.roll(y[:, 128:].reshape(COLS, 8, 128), 4, 1)
+        z = z * twist[p, t, 0][None] + pltpu.roll(z, 4, 1) * twist[p, t, 1][None]
+        swapped = swap_groups([z[c] for c in range(COLS)])
         for d in range(8):
-            outgoing[8 * t + d, :, :128] = swapped_real[d]
-            outgoing[8 * t + d, :, 128:] = swapped_imag[d]
-
+            outgoing[p, 8 * t + d] = swapped[d]
+
+    def send_tile(p, t):
         @pl.loop(0, 8)
         def _(j):
             device = 8 * t + (place + j) % 8
 
             @pl.when(device != place)
             def _():
-                send(device).start()
-
-    incoming[place] = outgoing[place]
-    everything = pltpu.make_async_remote_copy(
-        src_ref=outgoing.at[pl.ds(0, PEERS)],
-        dst_ref=incoming.at[pl.ds(0, PEERS)],
-        send_sem=all_sem.at[0],
-        recv_sem=all_sem.at[1],
-        device_id=(partner, col),
-        device_id_type=MESH,
-    )
-    loads[2].wait()
-    loads[3].wait()
-    everything.wait_recv()
-
-    held = incoming[...].reshape(POINTS, 256).T
-    rh, rl = split(held)
-    th, tl = oh[...], ol[...]
-    v = dot(rh, th) + (dot(rl, th) + dot(rh, tl))
-    real = (v[:128, :POINTS] - v[128:, POINTS:]).reshape(COLS, BLOCK, POINTS)
-    imag = (v[:128, POINTS:] + v[128:, :POINTS]).reshape(COLS, BLOCK, POINTS)
-    values[0] = real
-    values[1] = imag
-    store = pltpu.make_async_copy(values, evaluations, store_sem)
-    store.start()
+                send(p, device).start()
+
+    @pl.loop(0, TILES)
+    def _(i):
+        t = tile_of(i)
+        load_tile(t).wait()
+        run_tile(0, t)
+        send_tile(0, t)
+
+    incoming[half, place] = outgoing[0, place]
+    pair.wait_recv()
+    prepare(1, other)
+
+    @pl.loop(0, TILES)
+    def _(i):
+        t = tile_of(i)
+        run_tile(1, t)
+        send_tile(1, t)
+
+    incoming[1 - half, place] = outgoing[1, place]
+    load_outer.wait()
+
+    def finish(p):
+        whole(p).wait_recv()
+        part = (half + p) % 2
+        held = incoming[part].reshape(POINTS, 128).T
+        rh, rl = split(held)
+        th, tl = outer[part, 0], outer[part, 1]
+        return dot(rh, th) + (dot(rl, th) + dot(rh, tl))
+
+    v = finish(0)
+    v = v + finish(1)
+    real = v[:, :POINTS].reshape(COLS, BLOCK, POINTS)
+    imag = v[:, POINTS:].reshape(COLS, BLOCK, POINTS)
+    evaluations[0] = real
+    evaluations[1] = imag
 
     a1 = alpha[0]
     a2 = a1 * a1
@@ -323,15 +353,16 @@
     quotient[0] = (num_real * van_real + num_imag * van_imag) / denominator
     quotient[1] = (num_imag * van_real - num_real * van_imag) / denominator
 
-    everything.wait_send()
+    pair.wait_send()
+    whole(0).wait_send()
+    whole(1).wait_send()
     parts.wait_send()
     edges.wait_send()
-    store.wait()
 
 
 def per_device(coeffs, constraint_coeffs, alpha, coset_shift):
-    tables = inner_table() + outer_table()
-    any_space = pl.BlockSpec(memory_space=pl.ANY)
+    tables = inner_table(), outer_table()
+    hbm = pl.BlockSpec(memory_space=pltpu.HBM)
     vmem = pl.BlockSpec(memory_space=pltpu.VMEM)
     smem = pl.BlockSpec(memory_space=pltpu.SMEM)
     f32 = jnp.float32
@@ -342,33 +373,31 @@
             jax.ShapeDtypeStruct((2, COLS, BLOCK, POINTS), f32),
             jax.ShapeDtypeStruct((2, BLOCK, 128), f32),
         ),
-        in_specs=[vmem, smem, smem, smem] + [any_space] * 4,
-        out_specs=(any_space, vmem),
+        in_specs=[hbm, smem, smem, smem] + [hbm] * 2,
+        out_specs=(vmem, vmem),
         scratch_shapes=[
-            pltpu.VMEM((2, COLS, 4, K2), f32),
-            pltpu.VMEM((TILES, K2, 256), bf16),
-            pltpu.VMEM((TILES, K2, 256), bf16),
-            pltpu.VMEM((POINTS, 2 * POINTS), bf16),
-            pltpu.VMEM((POINTS, 2 * POINTS), bf16),
-            pltpu.VMEM((128, K2), bf16),
-            pltpu.VMEM((128, K2), bf16),
-            pltpu.VMEM((TILES, 2, 8, 128), f32),
-            pltpu.VMEM((HALF, 8, 256), f32),
-            pltpu.VMEM((HALF, 8, 256), f32),
-            pltpu.VMEM((2, COLS, BLOCK, POINTS), f32),
+            pltpu.VMEM((COLS, 4, K2), f32),
+            pltpu.VMEM((COLS, 4, K2), f32),
+            pltpu.VMEM((TILES, 2, K2, 256), bf16),
+            pltpu.VMEM((2, 2, POINTS, 2 * POINTS), bf16),
+            pltpu.VMEM((2, 2, 64, K2), bf16),
+            pltpu.VMEM((2, TILES, 2, 8, 128), f32),
+            pltpu.VMEM((2, HALF, 8, 128), f32),
+            pltpu.VMEM((2, HALF, 8, 128), f32),
             pltpu.VMEM((GROUPS, 2, BLOCK, 128), f32),
             pltpu.VMEM((GROUPS, 2, BLOCK, 128), f32),
             pltpu.VMEM((GROUPS, 8, 128), f32),
             pltpu.VMEM((GROUPS, 8, 128), f32),
-            pltpu.SemaphoreType.DMA((4,)),
+            pltpu.SemaphoreType.DMA((TILES + 1,)),
+            pltpu.SemaphoreType.DMA,
             pltpu.SemaphoreType.DMA((2,)),
             pltpu.SemaphoreType.DMA((2,)),
             pltpu.SemaphoreType.DMA((2,)),
             pltpu.SemaphoreType.DMA((2,)),
-            pltpu.SemaphoreType.DMA,
+            pltpu.SemaphoreType.DMA((2,)),
         ],
         compiler_params=pltpu.CompilerParams(
-            collective_id=0, has_side_effects=True, vmem_limit_bytes=48 * 1024 * 1024
+            collective_id=0, has_side_effects=True, vmem_limit_bytes=62 * 1024 * 1024
         ),
     )(coeffs, constraint_coeffs, alpha, coset_shift, *tables)
 

time: 53.2 us -> 44.9 us (0.84)
  Pallas kernels: 44 us -> 39.5 us
  local copies, waits for them, and re-layouts: 6.95 us -> 3.2 us
    pallas_call x1, Pallas kernels: 44 us -> 39.5 us  [per_device(): pl.pallas_call(kernel, out_shape=(jax.ShapeDtypeStruct((2, COLS, BLOCK, P...]
    unnamed x12 -> x2, local copies, waits for them, and re-layouts: 6.95 us -> 3.2 us
where the time goes in v1:
time: 44.9 us; the launch traced here: 44.7 us
  Pallas kernels  39.5 us (88%)
  local copies, waits for them, and re-layouts  3.2 us (7%)
  between operations  1.93 us (4%)
    pallas_call x1, Pallas kernels, per_device(): pl.pallas_call(kernel, out_shape=(jax.ShapeDtypeStruct((2, COLS, BLOCK, P...  39.5 us
    unnamed x2, local copies, waits for them, and re-layouts  3.2 us

profile of v1, /device:TPU:1, one launch (start us, length us, event | category | flops | bytes accessed | tf_op | source)
XLA Modules:
  0.0 44.7 jit_solution(2905596968819375377)
XLA Ops:
  1.9 39.5 %shard_map.77 = (f32[2,8,16,512]{3,2,1,0:T(8,128)}, f32[2,16,128]{2,1,0:T(8,128)}) custom-call(f32[8,4,512]{2,1,0:T(4,128)} %coeffs.1, f32[2,32]{1,0:T(2,128)} %constraint.1, f32[1]{0:T(128)S(6)} %copy.10.alpha, f32[1]{0:T(128)S(6)} %copy.11.coset, bf16[8,2,512,256]{3,2,1,0:T(8,128)(2,1)} %constant.4.clone.inner_hbm, ...), custom_call_target="tpu_custom_call" | custom-call | tf_op jit(solution)/shard_map/pallas_call | solution.py:370
  41.5 1.9 %copy.12 = f32[2,8,16,512]{3,2,1,0:T(8,128)} copy(f32[2,8,16,512]{3,2,1,0:T(8,128)} %get-tuple-element.4) | data formatting | bytes 1048576
  43.3 1.3 %copy.13 = f32[2,16,128]{2,1,0:T(8,128)} copy(f32[2,16,128]{2,1,0:T(8,128)} %get-tuple-element.5) | data formatting | bytes 32768

commit v2 on v1

--- a/solution.py
+++ b/solution.py
@@ -79,7 +79,7 @@
 
 def kernel(
     coeffs,
-    constraint,
+    constraint_hbm,
     alpha,
     coset,
     inner_hbm,
@@ -105,6 +105,8 @@
     recv_sem,
     part_sem,
     edge_sem,
+    constraint,
+    small_sem,
 ):
     row = lax.axis_index("row")
     col = lax.axis_index("col")
@@ -122,33 +124,32 @@
     def greet(device):
         pl.semaphore_signal(barrier, inc=1, device_id=device, device_id_type=MESH)
 
+    def tile_of(i):
+        offset = (i + 1) // 2 * (2 * ((i + 1) % 2) - 1)
+        return (tile + 4 + offset * (1 - 2 * core) + 8) % TILES
+
+    def load_tile(t):
+        return pltpu.make_async_copy(inner_hbm.at[t], inner.at[t], table_sem.at[t])
+
+    load_own = pltpu.make_async_copy(coeffs, own, own_sem)
+    load_own.start()
+    load_small = pltpu.make_async_copy(constraint_hbm, constraint, small_sem)
+    load_small.start()
+
+    @pl.loop(0, TILES)
+    def _(i):
+        load_tile(tile_of(i)).start()
+
+    load_outer = pltpu.make_async_copy(outer_hbm, outer, table_sem.at[TILES])
+    load_outer.start()
+
     greet((partner, col))
-
-    @pl.loop(1, HALF)
-    def _(i):
+    for i in range(1, HALF):
         greet((base + (place + i) % HALF, col))
-
     for i in range(1, GROUPS):
         greet((row, (col + i) % GROUPS))
     for i in range(GROUPS):
         greet((following, i))
-
-    def tile_of(i):
-        offset = (i + 1) // 2 * (2 * ((i + 1) % 2) - 1)
-        return (tile + 4 + offset * (1 - 2 * core) + 8) % TILES
-
-    def load_tile(t):
-        return pltpu.make_async_copy(inner_hbm.at[t], inner.at[t], table_sem.at[t])
-
-    load_own = pltpu.make_async_copy(coeffs, own, own_sem)
-    load_own.start()
-
-    @pl.loop(0, TILES)
-    def _(i):
-        load_tile(tile_of(i)).start()
-
-    load_outer = pltpu.make_async_copy(outer_hbm, outer, table_sem.at[TILES])
-    load_outer.start()
 
     shift = coset[0]
     k2 = lax.broadcasted_iota(jnp.int32, (1, K2), 1)
@@ -228,31 +229,33 @@
         for d in range(8):
             outgoing[p, 8 * t + d] = swapped[d]
 
-    def send_tile(p, t):
-        @pl.loop(0, 8)
-        def _(j):
-            device = 8 * t + (place + j) % 8
-
-            @pl.when(device != place)
-            def _():
-                send(p, device).start()
-
-    @pl.loop(0, TILES)
+    def send_tile(p, t, first):
+        for j in range(first, 8):
+            send(p, 8 * t + (place + j) % 8).start()
+
+    @pl.loop(0, TILES - 1)
     def _(i):
         t = tile_of(i)
         load_tile(t).wait()
         run_tile(0, t)
-        send_tile(0, t)
+        send_tile(0, t, 0)
+
+    load_tile(tile).wait()
+    run_tile(0, tile)
+    send_tile(0, tile, 1)
 
     incoming[half, place] = outgoing[0, place]
     pair.wait_recv()
     prepare(1, other)
 
-    @pl.loop(0, TILES)
+    @pl.loop(0, TILES - 1)
     def _(i):
         t = tile_of(i)
         run_tile(1, t)
-        send_tile(1, t)
+        send_tile(1, t, 0)
+
+    run_tile(1, tile)
+    send_tile(1, tile, 1)
 
     incoming[1 - half, place] = outgoing[1, place]
     load_outer.wait()
@@ -272,6 +275,7 @@
     evaluations[0] = real
     evaluations[1] = imag
 
+    load_small.wait()
     a1 = alpha[0]
     a2 = a1 * a1
     a4 = a2 * a2
@@ -361,7 +365,10 @@
 
 
 def per_device(coeffs, constraint_coeffs, alpha, coset_shift):
-    tables = inner_table(), outer_table()
+    def pinned(array):
+        return pltpu.with_memory_space_constraint(array, pltpu.HBM)
+
+    tables = [pinned(jnp.asarray(table)) for table in (inner_table(), outer_table())]
     hbm = pl.BlockSpec(memory_space=pltpu.HBM)
     vmem = pl.BlockSpec(memory_space=pltpu.VMEM)
     smem = pl.BlockSpec(memory_space=pltpu.SMEM)
@@ -373,7 +380,7 @@
             jax.ShapeDtypeStruct((2, COLS, BLOCK, POINTS), f32),
             jax.ShapeDtypeStruct((2, BLOCK, 128), f32),
         ),
-        in_specs=[hbm, smem, smem, smem] + [hbm] * 2,
+        in_specs=[hbm, hbm, smem, smem] + [hbm] * 2,
         out_specs=(vmem, vmem),
         scratch_shapes=[
             pltpu.VMEM((COLS, 4, K2), f32),
@@ -395,11 +402,19 @@
             pltpu.SemaphoreType.DMA((2,)),
             pltpu.SemaphoreType.DMA((2,)),
             pltpu.SemaphoreType.DMA((2,)),
+            pltpu.SMEM((2, GROUPS * COLS), f32),
+            pltpu.SemaphoreType.DMA,
         ],
         compiler_params=pltpu.CompilerParams(
-            collective_id=0, has_side_effects=True, vmem_limit_bytes=62 * 1024 * 1024
+            collective_id=0, has_side_effects=True, vmem_limit_bytes=48 * 1024 * 1024
         ),
-    )(coeffs, constraint_coeffs, alpha, coset_shift, *tables)
+    )(
+        pinned(coeffs),
+        pinned(constraint_coeffs),
+        alpha,
+        coset_shift,
+        *tables,
+    )
 
 
 def solution(mesh):

time: 44.9 us -> 41.6 us (0.927)
  local copies, waits for them, and re-layouts: 3.2 us -> 1.4 us
  Pallas kernels: 39.5 us -> 38.2 us
    unnamed x2, local copies, waits for them, and re-layouts: 3.2 us -> 1.4 us
    pallas_call x1, Pallas kernels: 39.5 us -> 38.2 us  [per_device(): pl.pallas_call(kernel, out_shape=(jax.ShapeDtypeStruct((2, COLS, BLOCK, P...]
where the time goes in v2:
time: 41.6 us; the launch traced here: 41.5 us
  Pallas kernels  38.2 us (92%)
  between operations  1.93 us (5%)
  local copies, waits for them, and re-layouts  1.4 us (3%)
    pallas_call x1, Pallas kernels, per_device(): pl.pallas_call(kernel, out_shape=(jax.ShapeDtypeStruct((2, COLS, BLOCK, P...  38.2 us
    unnamed x2, local copies, waits for them, and re-layouts  1.4 us

profile of v2, /device:TPU:1, one launch (start us, length us, event | category | flops | bytes accessed | tf_op | source)
XLA Modules:
  0.0 41.5 jit_solution(14127456453968715766)
XLA Ops:
  1.9 38.2 %shard_map.77 = (f32[2,8,16,512]{3,2,1,0:T(8,128)S(1)}, f32[2,16,128]{2,1,0:T(8,128)S(1)}) custom-call(f32[8,4,512]{2,1,0:T(4,128)} %coeffs.1, f32[2,32]{1,0:T(2,128)} %constraint_hbm.1, f32[1]{0:T(128)S(6)} %copy.10.alpha, f32[1]{0:T(128)S(6)} %copy.11.coset, bf16[8,2,512,256]{3,2,1,0:T(8,128)(2,1)} %constant.4.clone.inner_hbm, ...), custom_call_target="tpu_custom_call" | custom-call | tf_op jit(solution)/shard_map/pallas_call | solution.py:377
  40.1 0.8 %copy.12 = f32[2,8,16,512]{3,2,1,0:T(8,128)} copy(f32[2,8,16,512]{3,2,1,0:T(8,128)S(1)} %get-tuple-element.4) | data formatting | bytes 1048576
  40.9 0.6 %copy.13 = f32[2,16,128]{2,1,0:T(8,128)} copy(f32[2,16,128]{2,1,0:T(8,128)S(1)} %get-tuple-element.5) | data formatting | bytes 32768

commit v3 on v2

--- a/solution.py
+++ b/solution.py
@@ -22,7 +22,7 @@
 BLOCK = 16
 STEP = 4
 PEERS = HALF - 1
-BARRIER = PEERS + 1 + (GROUPS - 1) + GROUPS
+SOON_TILES = 3
 
 
 def split_table(table):
@@ -107,6 +107,12 @@
     edge_sem,
     constraint,
     small_sem,
+    pair_ready,
+    edge_ready,
+    run_ready,
+    extra,
+    beyond,
+    extra_sem,
 ):
     row = lax.axis_index("row")
     col = lax.axis_index("col")
@@ -125,8 +131,8 @@
         pl.semaphore_signal(barrier, inc=1, device_id=device, device_id_type=MESH)
 
     def tile_of(i):
-        offset = (i + 1) // 2 * (2 * ((i + 1) % 2) - 1)
-        return (tile + 4 + offset * (1 - 2 * core) + 8) % TILES
+        offset = (1 + (3 + 3 * i) % 7) * (1 - i // 7)
+        return (tile + offset * (1 - 2 * core) + 8) % TILES
 
     def load_tile(t):
         return pltpu.make_async_copy(inner_hbm.at[t], inner.at[t], table_sem.at[t])
@@ -143,24 +149,50 @@
     load_outer = pltpu.make_async_copy(outer_hbm, outer, table_sem.at[TILES])
     load_outer.start()
 
-    greet((partner, col))
-    for i in range(1, HALF):
-        greet((base + (place + i) % HALF, col))
+    first_half = half == 0
+    first_row = row == 0
+    last_row = row == ROWS - 1
+
+    @pl.when(first_half)
+    def _():
+        greet((partner, col))
+
+    seat = place % 8
+
+    def in_line(i):
+        return base + (tile + i) % TILES * 8 + seat
+
+    for i in range(1, TILES):
+        greet((base + 8 * tile + (place + i) % 8, col))
+        greet((in_line(i), col))
     for i in range(1, GROUPS):
         greet((row, (col + i) % GROUPS))
-    for i in range(GROUPS):
-        greet((following, i))
+
+    @pl.when((row != PEERS) & (row != ROWS - 1))
+    def _():
+        for i in range(GROUPS):
+            greet((following, i))
+
+    @pl.when(first_row)
+    def _():
+        for i in range(GROUPS):
+            greet((previous, i))
+
+    expected = 2 * (TILES - 1) + GROUPS - 1 + half
+    expected = expected + jnp.where(place == 0, 0, GROUPS) + jnp.where(last_row, GROUPS, 0)
 
     shift = coset[0]
     k2 = lax.broadcasted_iota(jnp.int32, (1, K2), 1)
     phase = k2.astype(jnp.float32) * (shift * (TAU / 2048))
     sign = (1 - 2 * ((k2 % 2) * half)).astype(jnp.float32)
+    turn = (1 - 2 * (k2 % 2)).astype(jnp.float32)
     phase_cos = jnp.cos(phase) * sign
     phase_sin = jnp.sin(phase) * sign
 
-    sub = lax.broadcasted_iota(jnp.int32, (8, 1024), 0)
+    wide = 128 * (TILES + 1)
+    sub = lax.broadcasted_iota(jnp.int32, (8, wide), 0)
     k1 = 256 * ((half + sub // 4) % 2) + 4 * place + sub % 4
-    point = 1024 * half + lax.broadcasted_iota(jnp.int32, (8, 1024), 1)
+    point = 1024 * half + lax.broadcasted_iota(jnp.int32, (8, wide), 1)
     k1_f = k1.astype(jnp.float32)
     angle = ((k1 * point).astype(jnp.float32) + k1_f * shift) * (TAU / 1048576)
     cosine, sine = jnp.cos(angle), jnp.sin(angle)
@@ -171,7 +203,7 @@
         (jnp.where(upper, cosine_turned, cosine), jnp.where(upper, -sine_turned, sine)),
     )
     for p in range(2):
-        for t in range(TILES):
+        for t in range(TILES + 1):
             twist[p, t, 0] = pairs[p][0][:, 128 * t : 128 * t + 128]
             twist[p, t, 1] = pairs[p][1][:, 128 * t : 128 * t + 128]
 
@@ -181,10 +213,13 @@
         high, low = split(x)
         x_split[p, 0] = high
         x_split[p, 1] = low
+        high, low = split(x * turn)
+        x_split[2 + p, 0] = high
+        x_split[2 + p, 1] = low
 
     load_own.wait()
     prepare(0, own)
-    pl.semaphore_wait(barrier, BARRIER)
+    pl.semaphore_wait(barrier, expected)
 
     pair = pltpu.make_async_remote_copy(
         src_ref=coeffs,
@@ -194,57 +229,97 @@
         device_id=(partner, col),
         device_id_type=MESH,
     )
-    pair.start()
-
-    def send(p, device):
+
+    @pl.when(half == 1)
+    def _():
+        pl.semaphore_signal(pair_ready, inc=1, device_id=(partner, col), device_id_type=MESH)
+        pair.start()
+
+    for i in range(1, TILES):
+        pl.semaphore_signal(run_ready, inc=1, device_id=(in_line(i), col), device_id_type=MESH)
+
+    @pl.when(last_row)
+    def _():
+        for i in range(GROUPS):
+            pl.semaphore_signal(edge_ready, inc=1, device_id=(following, i), device_id_type=MESH)
+
+    def send(source, target, device, sem):
         return pltpu.make_async_remote_copy(
-            src_ref=outgoing.at[p, device],
-            dst_ref=incoming.at[(half + p) % 2, place],
-            send_sem=send_sem.at[p],
-            recv_sem=recv_sem.at[p],
+            src_ref=source,
+            dst_ref=target,
+            send_sem=send_sem.at[sem],
+            recv_sem=recv_sem.at[sem],
             device_id=(base + device, col),
             device_id_type=MESH,
         )
 
-    def whole(p):
+    def send_extra(part):
         return pltpu.make_async_remote_copy(
-            src_ref=outgoing.at[p, pl.ds(0, PEERS)],
-            dst_ref=incoming.at[(half + p) % 2, pl.ds(0, PEERS)],
-            send_sem=send_sem.at[p],
-            recv_sem=recv_sem.at[p],
-            device_id=(partner, col),
+            src_ref=outgoing.at[HALF, part],
+            dst_ref=extra.at[place, part],
+            send_sem=extra_sem.at[0, part],
+            recv_sem=extra_sem.at[1, 0],
+            device_id=(base + PEERS, col),
             device_id_type=MESH,
         )
 
+    def blocks(sem):
+        where = (pl.ds(0, PEERS), 0)
+        return send(outgoing.at[where], incoming.at[where], (place + 1) % HALF, sem)
+
     minus = jnp.where(lax.broadcasted_iota(jnp.int32, (1, 8, 128), 1) < 4, -1.0, 1.0)
 
-    def run_tile(p, t):
-        ah, al = x_split[p, 0], x_split[p, 1]
+    def tile_blocks(x, t, p, turned):
+        ah, al = x_split[x, 0], x_split[x, 1]
         bh, bl = inner[t, 0], inner[t, 1]
         y = dot(ah, bh) + (dot(al, bh) + dot(ah, bl))
         z = y[:, :128].reshape(COLS, 8, 128)
         z = z + minus * pltpu.roll(y[:, 128:].reshape(COLS, 8, 128), 4, 1)
-        z = z * twist[p, t, 0][None] + pltpu.roll(z, 4, 1) * twist[p, t, 1][None]
-        swapped = swap_groups([z[c] for c in range(COLS)])
-        for d in range(8):
-            outgoing[p, 8 * t + d] = swapped[d]
+        z = z * twist[p, turned, 0][None] + pltpu.roll(z, 4, 1) * twist[p, turned, 1][None]
+        return swap_groups([z[c] for c in range(COLS)])
+
+    def run_tile(p, t):
+        for d, block in enumerate(tile_blocks(p, t, p, t)):
+            outgoing[8 * t + d, (half + p) % 2] = block
 
     def send_tile(p, t, first):
+        part = (half + p) % 2
         for j in range(first, 8):
-            send(p, 8 * t + (place + j) % 8).start()
-
-    @pl.loop(0, TILES - 1)
-    def _(i):
+            device = 8 * t + (place + j) % 8
+            send(outgoing.at[device, part], incoming.at[place, part], device, p).start()
+
+    def extra_tile(p):
+        part = (half + p) % 2
+        outgoing[HALF, part] = tile_blocks(2 + p, 0, p, TILES)[0]
+
+        @pl.when(place < PEERS)
+        def _():
+            send_extra(part).start()
+
+    pl.semaphore_wait(run_ready, TILES - 1)
+
+    def own_tile(i):
         t = tile_of(i)
         load_tile(t).wait()
         run_tile(0, t)
         send_tile(0, t, 0)
 
+    pl.loop(0, SOON_TILES)(own_tile)
+
+    @pl.when(first_half)
+    def _():
+        pl.semaphore_wait(pair_ready, 1)
+        pair.start()
+
+    pl.loop(SOON_TILES, TILES - 1)(own_tile)
     load_tile(tile).wait()
     run_tile(0, tile)
     send_tile(0, tile, 1)
 
-    incoming[half, place] = outgoing[0, place]
+    @pl.when(first_half)
+    def _():
+        extra_tile(0)
+
     pair.wait_recv()
     prepare(1, other)
 
@@ -254,22 +329,40 @@
         run_tile(1, t)
         send_tile(1, t, 0)
 
+    @pl.when(first_half)
+    def _():
+        extra_tile(1)
+
     run_tile(1, tile)
     send_tile(1, tile, 1)
-
-    incoming[1 - half, place] = outgoing[1, place]
+    incoming[place] = outgoing[place]
     load_outer.wait()
 
-    def finish(p):
-        whole(p).wait_recv()
-        part = (half + p) % 2
-        held = incoming[part].reshape(POINTS, 128).T
+    def finish(blocks_in, part):
+        held = blocks_in[:, part].reshape(POINTS, 128).T
         rh, rl = split(held)
         th, tl = outer[part, 0], outer[part, 1]
         return dot(rh, th) + (dot(rl, th) + dot(rh, tl))
 
-    v = finish(0)
-    v = v + finish(1)
+    @pl.when(half == 1)
+    def _():
+        blocks(1).wait_recv()
+
+    @pl.when(first_half)
+    def _():
+        blocks(0).wait_recv()
+
+    v = finish(incoming, 0)
+
+    @pl.when(half == 1)
+    def _():
+        blocks(0).wait_recv()
+
+    @pl.when(first_half)
+    def _():
+        blocks(1).wait_recv()
+
+    v = v + finish(incoming, 1)
     real = v[:, :POINTS].reshape(COLS, BLOCK, POINTS)
     imag = v[:, POINTS:].reshape(COLS, BLOCK, POINTS)
     evaluations[0] = real
@@ -281,6 +374,7 @@
     a4 = a2 * a2
     a8 = a4 * a4
     weight = jnp.where(col % 2 == 1, a8, 1.0) * jnp.where(col // 2 == 1, a8 * a8, 1.0)
+    first_weight = weight
     ahead_real = ahead_imag = sum_real = sum_imag = 0.0
     for c in range(COLS):
         quad = constraint[0, COLS * col + c]
@@ -292,9 +386,31 @@
         sum_imag += weight * (quad * (2.0 * vr * vi) + linear * vi)
         weight = weight * a1
 
-    none = jnp.zeros((STEP, POINTS), jnp.float32)
-    sum_real = jnp.concatenate((ahead_real[STEP:], none), axis=0) - sum_real
-    sum_imag = jnp.concatenate((ahead_imag[STEP:], none), axis=0) - sum_imag
+    beyond[...] = jnp.zeros((2, STEP, POINTS), jnp.float32)
+
+    @pl.when(row == PEERS)
+    def _():
+        extra[place] = outgoing[HALF]
+        received = pltpu.make_async_remote_copy(
+            src_ref=outgoing.at[pl.ds(0, PEERS)],
+            dst_ref=extra.at[pl.ds(0, PEERS)],
+            send_sem=extra_sem.at[0, 0],
+            recv_sem=extra_sem.at[1, 0],
+            device_id=(base, col),
+            device_id_type=MESH,
+        )
+        received.wait_recv()
+        u = finish(extra, 0) + finish(extra, 1)
+        edge_in[...] = jnp.zeros((GROUPS, 8, 128), jnp.float32)
+        scale = first_weight
+        for c in range(COLS):
+            for p in range(2):
+                found = u[BLOCK * c : BLOCK * c + 8, POINTS * p : POINTS * (p + 1)]
+                beyond[p] += scale * found[:STEP]
+            scale = scale * a1
+
+    sum_real = jnp.concatenate((ahead_real[STEP:], beyond[0]), axis=0) - sum_real
+    sum_imag = jnp.concatenate((ahead_imag[STEP:], beyond[1]), axis=0) - sum_imag
     edge = jnp.concatenate((ahead_real[:STEP], ahead_imag[:STEP]), axis=0)
     edge = jnp.where(row == 0, pltpu.roll(edge, POINTS - 1, 1), edge)
     for q in range(GROUPS):
@@ -314,15 +430,23 @@
 
     for i in range(1, GROUPS):
         send_part((col + i) % GROUPS).start()
-    for q in range(GROUPS):
-        pltpu.make_async_remote_copy(
-            src_ref=edge_out.at[q],
-            dst_ref=edge_in.at[col],
-            send_sem=edge_sem.at[0],
-            recv_sem=edge_sem.at[1],
-            device_id=(previous, q),
-            device_id_type=MESH,
-        ).start()
+
+    @pl.when(first_row)
+    def _():
+        pl.semaphore_wait(edge_ready, GROUPS)
+
+    @pl.when(row != HALF)
+    def _():
+        for q in range(GROUPS):
+            pltpu.make_async_remote_copy(
+                src_ref=edge_out.at[q],
+                dst_ref=edge_in.at[col],
+                send_sem=edge_sem.at[0],
+                recv_sem=edge_sem.at[1],
+                device_id=(previous, q),
+                device_id_type=MESH,
+            ).start()
+
     part_in[col] = part_out[col]
 
     point = lax.broadcasted_iota(jnp.int32, (BLOCK, 128), 0) % STEP
@@ -348,7 +472,11 @@
         device_id_type=MESH,
     )
     parts.wait_recv()
-    edges.wait_recv()
+
+    @pl.when(row != PEERS)
+    def _():
+        edges.wait_recv()
+
     part = (part_in[0] + part_in[1]) + (part_in[2] + part_in[3])
     edge = (edge_in[0] + edge_in[1]) + (edge_in[2] + edge_in[3])
     none = jnp.zeros((BLOCK - STEP, 128), jnp.float32)
@@ -358,10 +486,19 @@
     quotient[1] = (num_imag * van_real - num_real * van_imag) / denominator
 
     pair.wait_send()
-    whole(0).wait_send()
-    whole(1).wait_send()
+    blocks(0).wait_send()
+    blocks(1).wait_send()
+
+    @pl.when(first_half & (place < PEERS))
+    def _():
+        send_extra(0).wait_send()
+        send_extra(1).wait_send()
+
     parts.wait_send()
-    edges.wait_send()
+
+    @pl.when(row != HALF)
+    def _():
+        edges.wait_send()
 
 
 def per_device(coeffs, constraint_coeffs, alpha, coset_shift):
@@ -387,10 +524,10 @@
             pltpu.VMEM((COLS, 4, K2), f32),
             pltpu.VMEM((TILES, 2, K2, 256), bf16),
             pltpu.VMEM((2, 2, POINTS, 2 * POINTS), bf16),
-            pltpu.VMEM((2, 2, 64, K2), bf16),
-            pltpu.VMEM((2, TILES, 2, 8, 128), f32),
-            pltpu.VMEM((2, HALF, 8, 128), f32),
-            pltpu.VMEM((2, HALF, 8, 128), f32),
+            pltpu.VMEM((4, 2, 64, K2), bf16),
+            pltpu.VMEM((2, TILES + 1, 2, 8, 128), f32),
+            pltpu.VMEM((HALF + 1, 2, 8, 128), f32),
+            pltpu.VMEM((HALF, 2, 8, 128), f32),
             pltpu.VMEM((GROUPS, 2, BLOCK, 128), f32),
             pltpu.VMEM((GROUPS, 2, BLOCK, 128), f32),
             pltpu.VMEM((GROUPS, 8, 128), f32),
@@ -404,6 +541,12 @@
             pltpu.SemaphoreType.DMA((2,)),
             pltpu.SMEM((2, GROUPS * COLS), f32),
             pltpu.SemaphoreType.DMA,
+            pltpu.SemaphoreType.REGULAR,
+            pltpu.SemaphoreType.REGULAR,
+            pltpu.SemaphoreType.REGULAR,
+            pltpu.VMEM((HALF, 2, 8, 128), f32),
+            pltpu.VMEM((2, STEP, POINTS), f32),
+            pltpu.SemaphoreType.DMA((2, 2)),
         ],
         compiler_params=pltpu.CompilerParams(
             collective_id=0, has_side_effects=True, vmem_limit_bytes=48 * 1024 * 1024

time: 41.6 us -> 40.5 us (0.974)
  Pallas kernels: 38.2 us -> 37 us
    pallas_call x1, Pallas kernels: 38.2 us -> 37 us  [per_device(): pl.pallas_call(kernel, out_shape=(jax.ShapeDtypeStruct((2, COLS, BLOCK, P...]
where the time goes in v3:
time: 40.5 us; the launch traced here: 40.4 us
  Pallas kernels  37 us (91%)
  between operations  1.93 us (5%)
  local copies, waits for them, and re-layouts  1.4 us (3%)
    pallas_call x1, Pallas kernels, per_device(): pl.pallas_call(kernel, out_shape=(jax.ShapeDtypeStruct((2, COLS, BLOCK, P...  37 us
    unnamed x2, local copies, waits for them, and re-layouts  1.4 us

profile of v3, /device:TPU:1, one launch (start us, length us, event | category | flops | bytes accessed | tf_op | source)
XLA Modules:
  0.0 40.4 jit_solution(13132278509643249424)
XLA Ops:
  1.9 37.0 %shard_map.77 = (f32[2,8,16,512]{3,2,1,0:T(8,128)S(1)}, f32[2,16,128]{2,1,0:T(8,128)S(1)}) custom-call(f32[8,4,512]{2,1,0:T(4,128)} %coeffs.1, f32[2,32]{1,0:T(2,128)} %constraint_hbm.1, f32[1]{0:T(128)S(6)} %copy.10.alpha, f32[1]{0:T(128)S(6)} %copy.11.coset, bf16[8,2,512,256]{3,2,1,0:T(8,128)(2,1)} %constant.4.clone.inner_hbm, ...), custom_call_target="tpu_custom_call" | custom-call | tf_op jit(solution)/shard_map/pallas_call | solution.py:514
  39.0 0.8 %copy.12 = f32[2,8,16,512]{3,2,1,0:T(8,128)} copy(f32[2,8,16,512]{3,2,1,0:T(8,128)S(1)} %get-tuple-element.4) | data formatting | bytes 1048576
  39.8 0.6 %copy.13 = f32[2,16,128]{2,1,0:T(8,128)} copy(f32[2,16,128]{2,1,0:T(8,128)S(1)} %get-tuple-element.5) | data formatting | bytes 32768

commit v4 on v3

--- a/solution.py
+++ b/solution.py
@@ -22,7 +22,6 @@
 BLOCK = 16
 STEP = 4
 PEERS = HALF - 1
-SOON_TILES = 3
 
 
 def split_table(table):
@@ -304,14 +303,7 @@
         run_tile(0, t)
         send_tile(0, t, 0)
 
-    pl.loop(0, SOON_TILES)(own_tile)
-
-    @pl.when(first_half)
-    def _():
-        pl.semaphore_wait(pair_ready, 1)
-        pair.start()
-
-    pl.loop(SOON_TILES, TILES - 1)(own_tile)
+    pl.loop(0, TILES - 1)(own_tile)
     load_tile(tile).wait()
     run_tile(0, tile)
     send_tile(0, tile, 1)
@@ -319,6 +311,8 @@
     @pl.when(first_half)
     def _():
         extra_tile(0)
+        pl.semaphore_wait(pair_ready, 1)
+        pair.start()
 
     pair.wait_recv()
     prepare(1, other)
@@ -329,12 +323,13 @@
         run_tile(1, t)
         send_tile(1, t, 0)
 
-    @pl.when(first_half)
-    def _():
-        extra_tile(1)
-
     run_tile(1, tile)
     send_tile(1, tile, 1)
+
+    @pl.when(first_half)
+    def _():
+        extra_tile(1)
+
     incoming[place] = outgoing[place]
     load_outer.wait()
 
@@ -365,8 +360,6 @@
     v = v + finish(incoming, 1)
     real = v[:, :POINTS].reshape(COLS, BLOCK, POINTS)
     imag = v[:, POINTS:].reshape(COLS, BLOCK, POINTS)
-    evaluations[0] = real
-    evaluations[1] = imag
 
     load_small.wait()
     a1 = alpha[0]
@@ -448,6 +441,8 @@
             ).start()
 
     part_in[col] = part_out[col]
+    evaluations[0] = real
+    evaluations[1] = imag
 
     point = lax.broadcasted_iota(jnp.int32, (BLOCK, 128), 0) % STEP
     theta = (shift + point.astype(jnp.float32)) * (TAU / STEP)

time: 40.5 us -> 39.4 us (0.973)
  Pallas kernels: 37 us -> 35.9 us
    pallas_call x1, Pallas kernels: 37 us -> 35.9 us  [per_device(): pl.pallas_call(kernel, out_shape=(jax.ShapeDtypeStruct((2, COLS, BLOCK, P...]
where the time goes in v4:
time: 39.4 us; the launch traced here: 39.2 us
  Pallas kernels  35.9 us (91%)
  between operations  1.93 us (5%)
  local copies, waits for them, and re-layouts  1.4 us (4%)
    pallas_call x1, Pallas kernels, per_device(): pl.pallas_call(kernel, out_shape=(jax.ShapeDtypeStruct((2, COLS, BLOCK, P...  35.9 us
    unnamed x2, local copies, waits for them, and re-layouts  1.4 us

profile of v4, /device:TPU:1, one launch (start us, length us, event | category | flops | bytes accessed | tf_op | source)
XLA Modules:
  0.0 39.2 jit_solution(9252640138717975779)
XLA Ops:
  1.9 35.9 %shard_map.77 = (f32[2,8,16,512]{3,2,1,0:T(8,128)S(1)}, f32[2,16,128]{2,1,0:T(8,128)S(1)}) custom-call(f32[8,4,512]{2,1,0:T(4,128)} %coeffs.1, f32[2,32]{1,0:T(2,128)} %constraint_hbm.1, f32[1]{0:T(128)S(6)} %copy.10.alpha, f32[1]{0:T(128)S(6)} %copy.11.coset, bf16[8,2,512,256]{3,2,1,0:T(8,128)(2,1)} %constant.4.clone.inner_hbm, ...), custom_call_target="tpu_custom_call" | custom-call | tf_op jit(solution)/shard_map/pallas_call | solution.py:509
  37.8 0.8 %copy.12 = f32[2,8,16,512]{3,2,1,0:T(8,128)} copy(f32[2,8,16,512]{3,2,1,0:T(8,128)S(1)} %get-tuple-element.4) | data formatting | bytes 1048576
  38.6 0.6 %copy.13 = f32[2,16,128]{2,1,0:T(8,128)} copy(f32[2,16,128]{2,1,0:T(8,128)S(1)} %get-tuple-element.5) | data formatting | bytes 32768

commit v5 on v4

--- a/solution.py
+++ b/solution.py
@@ -212,16 +212,13 @@
         high, low = split(x)
         x_split[p, 0] = high
         x_split[p, 1] = low
-        high, low = split(x * turn)
-        x_split[2 + p, 0] = high
-        x_split[2 + p, 1] = low
 
     load_own.wait()
     prepare(0, own)
     pl.semaphore_wait(barrier, expected)
 
     pair = pltpu.make_async_remote_copy(
-        src_ref=coeffs,
+        src_ref=own,
         dst_ref=other,
         send_sem=pair_sem.at[0],
         recv_sem=pair_sem.at[1],
@@ -231,8 +228,8 @@
 
     @pl.when(half == 1)
     def _():
+        pair.start()
         pl.semaphore_signal(pair_ready, inc=1, device_id=(partner, col), device_id_type=MESH)
-        pair.start()
 
     for i in range(1, TILES):
         pl.semaphore_signal(run_ready, inc=1, device_id=(in_line(i), col), device_id_type=MESH)
@@ -289,6 +286,8 @@
 
     def extra_tile(p):
         part = (half + p) % 2
+        for level in range(2):
+            x_split[2 + p, level] = x_split[p, level] * turn.astype(jnp.bfloat16)
         outgoing[HALF, part] = tile_blocks(2 + p, 0, p, TILES)[0]
 
         @pl.when(place < PEERS)

time: 39.4 us -> 39.3 us (level)
  no operation moved by 1% of the time
where the time goes in v5:
time: 39.3 us; the launch traced here: 39.2 us
  Pallas kernels  35.8 us (91%)
  between operations  1.93 us (5%)
  local copies, waits for them, and re-layouts  1.4 us (4%)
    pallas_call x1, Pallas kernels, per_device(): pl.pallas_call(kernel, out_shape=(jax.ShapeDtypeStruct((2, COLS, BLOCK, P...  35.8 us
    unnamed x2, local copies, waits for them, and re-layouts  1.4 us

profile of v5, /device:TPU:1, one launch (start us, length us, event | category | flops | bytes accessed | tf_op | source)
XLA Modules:
  0.0 39.2 jit_solution(5126276833901278036)
XLA Ops:
  1.9 35.8 %shard_map.77 = (f32[2,8,16,512]{3,2,1,0:T(8,128)S(1)}, f32[2,16,128]{2,1,0:T(8,128)S(1)}) custom-call(f32[8,4,512]{2,1,0:T(4,128)} %coeffs.1, f32[2,32]{1,0:T(2,128)} %constraint_hbm.1, f32[1]{0:T(128)S(6)} %copy.10.alpha, f32[1]{0:T(128)S(6)} %copy.11.coset, bf16[8,2,512,256]{3,2,1,0:T(8,128)(2,1)} %constant.4.clone.inner_hbm, ...), custom_call_target="tpu_custom_call" | custom-call | tf_op jit(solution)/shard_map/pallas_call | solution.py:508
  37.8 0.8 %copy.12 = f32[2,8,16,512]{3,2,1,0:T(8,128)} copy(f32[2,8,16,512]{3,2,1,0:T(8,128)S(1)} %get-tuple-element.4) | data formatting | bytes 1048576
  38.6 0.6 %copy.13 = f32[2,16,128]{2,1,0:T(8,128)} copy(f32[2,16,128]{2,1,0:T(8,128)S(1)} %get-tuple-element.5) | data formatting | bytes 32768
